TPU v7x, 512 devices: a whole 4x8x8 slice. The times are simulated.
512 devices in a mesh: ctx: 32 (over x, z), exp: 16 (over y, core).
Axes of the slice: x: 4, y: 8, z: 8, core: 2. Of those that a mesh axis runs over, the one named last changes fastest.
Arguments:
- q_spikes: bfloat16 [16384, 4096], P('ctx', 'exp'), may hold values from -1 to 1, as said below
- k_spikes: bfloat16 [16384, 4096], P('ctx', 'exp'), may hold values from -1 to 1, as said below
- v_spikes: bfloat16 [16384, 4096], P('ctx', 'exp'), may hold values from -1 to 1, as said below
- log_decay: float32 [16384, 32], P('ctx', 'exp'), may hold values from -1 to 0, as said below
- norm_gain: float32 [4096], P('exp'), may hold values from 0.1 to 1.9
- out_weight: bfloat16 [4096, 4096], P('exp'), may hold values from -0.09375 to 0.09375
- residual: bfloat16 [16384, 4096], P(('ctx', 'exp')), may hold values from -6 to 6
Outputs:
- mixed: bfloat16 [16384, 4096], P(('ctx', 'exp'))
Inputs may be any that keep to these rules, and one draw needn't show every extreme that they name: `q_spikes`: every entry is -1, 0 or 1. `k_spikes`: every entry is -1, 0 or 1. `v_spikes`: every entry is -1, 0 or 1. `log_decay`: every entry is negative.
All inputs are finite; a program needn't handle non-finite values.
Results may differ from a plain program's by a relative error of at most 0.015.
Values may be sent and summed in bfloat16 or wider, within the bound.
A program may use at most 64 MiB of HBM per device.

v0:
```python
import jax
import jax.numpy as jnp
from jax import lax
from jax.sharding import PartitionSpec as P

HIGH = lax.Precision.HIGHEST


def entering(shard, axis, join, neutral):
    place = lax.axis_index(axis)
    gathered = jax.tree.map(
        lambda a, kind: lax.all_gather(a.astype(kind), axis), shard, (jnp.bfloat16, jnp.bfloat16)
    )
    state = jax.tree.map(lambda a, e: jnp.zeros_like(a) + jnp.asarray(e, a.dtype), shard, neutral)

    def one(lap, state):
        return join(
            state,
            jax.tree.map(
                lambda a, own: lax.dynamic_index_in_dim(a, lap, 0, False).astype(own.dtype),
                gathered,
                shard,
            ),
        )

    return lax.fori_loop(0, place, one, state)


def shards(q_spikes, k_spikes, v_spikes, log_decay, norm_gain, out_weight, residual):
    rows = q_spikes.shape[0]
    heads = log_decay.shape[1]
    width = q_spikes.shape[1] // heads
    query = q_spikes.astype(jnp.float32).reshape(rows, heads, width)
    key = k_spikes.astype(jnp.float32).reshape(rows, heads, width)
    value = v_spikes.astype(jnp.float32).reshape(rows, heads, width)
    cum = jnp.cumsum(log_decay, axis=0)
    place = jnp.arange(rows)
    causal = place[:, None] >= place[None, :]
    spread = cum[:, None, :] - cum[None, :, :]
    weight = jnp.exp(jnp.where(causal[:, :, None], spread, -jnp.inf))
    scores = jnp.einsum("thd,shd->tsh", query, key, precision=HIGH) * weight
    local = jnp.einsum("tsh,she->the", scores, value, precision=HIGH)
    total = cum[-1]
    keyed = key * jnp.exp(total[None, :] - cum)[:, :, None]
    own_state = jnp.einsum("shd,she->hde", keyed, value, precision=HIGH)
    empty = jnp.zeros((heads, width, width), jnp.float32)

    def combine(earlier, later):
        return (earlier[0] + later[0], earlier[1] * jnp.exp(later[0])[:, None, None] + later[1])

    decay_in, state_in = entering(
        (total, own_state), "ctx", combine, (jnp.zeros((heads,), jnp.float32), empty)
    )
    carried = jnp.einsum("thd,hde->the", query, state_in, precision=HIGH) * jnp.exp(cum)[:, :, None]
    attended = local + carried
    scale = jnp.sqrt(jnp.mean(attended * attended, axis=-1, keepdims=True) + 1e-06)
    normed = (
        (attended / scale * norm_gain.reshape(heads, width))
        .astype(jnp.bfloat16)
        .reshape(rows, heads * width)
    )
    summed = lax.psum_scatter(
        jnp.dot(normed, out_weight, preferred_element_type=jnp.float32).astype(jnp.bfloat16),
        "exp",
        scatter_dimension=0,
        tiled=True,
    ).astype(jnp.float32)
    return (summed + residual.astype(jnp.float32)).astype(jnp.bfloat16)


def solution(mesh):
    in_specs = (
        P("ctx", "exp"),
        P("ctx", "exp"),
        P("ctx", "exp"),
        P("ctx", "exp"),
        P("exp"),
        P("exp", None),
        P(("ctx", "exp"), None),
    )
    out_specs = P(("ctx", "exp"), None)
    return jax.shard_map(shards, mesh=mesh, in_specs=in_specs, out_specs=out_specs, check_vma=False)
```

profile of v0, /device:TPU:1, one launch (start us, length us, event | category | flops | bytes accessed | tf_op | source)
XLA Modules:
  0.0 208.2 jit_solution(3850762987392696712)
XLA Ops:
  6.5 0.0 copy-start
  6.5 0.0 all-gather.4.cloned.1.call-start
  6.5 0.8 reshape.62
  7.4 0.6 reduce-window.6
  8.0 0.2 slice_reduce_fusion
  8.2 0.2 reduce-window.9
  8.3 0.1 add_bitcast_fusion
  8.4 0.2 slice_reduce_fusion.1
  8.6 0.1 fusion.25
  8.7 0.0 copy-start.4
  8.7 1.1 copy.70
  9.8 2.0 convolution_convert_fusion.1
  11.8 0.0 all-gather.4.cloned.1.call-update
  11.8 0.0 reduce-scatter.2.cloned.1.call-start
  11.9 0.2 fusion.23
  12.1 37.6 %all-gather.1 = bf16[32,1,2]{2,1,0:T(2,128)(2,1)S(1)} all-gather(bf16[1,1,2]{2,1,0:T(2,128)(2,1)S(1)} %bitcast.87), channel_id=1, replica_groups=mesh['ctx'=32,'exp'=16] {'ctx'}, dimensions={0}, use_global_device_ids=true | all-gather | bytes 132 | tf_op jit(solution)/shard_map/all_gather | solution.py:12
  49.6 0.1 copy.61
  49.7 0.1 iota_compare_fusion
  49.8 1.4 fusion.16
  51.3 0.0 copy-done.4
  51.3 0.0 copy-start.1
  51.3 1.5 fusion.4
  52.8 0.0 copy-start.3
  52.8 44.7 %all-gather.4.cloned.1.call-done = bf16[64,128,128]{2,1,0:T(8,128)(2,1)} async-done(((bf16[2,128,128]{2,1,0:T(8,128)(2,1)}), bf16[64,128,128]{2,1,0:T(8,128)(2,1)}) %all-gather.4.cloned.1.call-update) | async-done | bytes 2097168 | tf_op jit(solution)/shard_map/all_gather | solution.py:12
  97.5 0.0 copy-done.1
  97.5 0.5 multiply_reduce_fusion
  98.0 0.0 copy-done.3
  98.0 0.1 multiply_convert_fusion
  98.1 0.0 copy-done
  98.1 3.2 %convolution_convert_fusion = bf16[512,4096]{1,0:T(8,128)(2,1)} fusion(bf16[512,256]{0,1:T(8,128)(2,1)S(1)} %bitcast.78, bf16[256,4096]{1,0:T(8,128)(2,1)S(1)} %copy-done), kind=kOutput, calls=%fused_computation.3 | convolution fusion | flops 1075838976 | bytes 6553600 | tf_op jit(solution)/shard_map/dot_general | solution.py:63
  101.3 0.0 copy-start.2
  101.3 0.0 reduce-scatter.2.cloned.1.call-update
  101.4 98.3 %reduce-scatter.2.cloned.1.call-done = bf16[32,4096]{1,0:T(8,128)(2,1)} async-done(((bf16[512,4096]{1,0:T(8,128)(2,1)}), bf16[32,4096]{1,0:T(8,128)(2,1)}) %reduce-scatter.2.cloned.1.call-update) | async-done | bytes 262160 | tf_op jit(solution)/shard_map/reduce_scatter | solution.py:62
  199.6 0.0 copy-done.2
  199.6 1.7 add_convert_fusion
  (4 shorter events, 0.0 us)
Async XLA Ops:
  6.5 91.6 %copy-start = (bf16[256,4096]{1,0:T(8,128)(2,1)S(1)}, bf16[256,4096]{1,0:T(8,128)(2,1)}, u32[]{:S(2)}) copy-start(bf16[256,4096]{1,0:T(8,128)(2,1)} %param.14) | copy-start | bytes 6291460
  6.5 90.9 %all-gather.4.cloned.1.call-start = ((), (), s32[]{:S(2)}) async-start(), calls=%async_computation.2 | async-start | bytes 2162688 | tf_op jit(solution)/shard_map/all_gather | solution.py:12
  8.7 42.6 %copy-start.4 = (bf16[512,256]{1,0:T(8,128)(2,1)S(1)}, bf16[512,256]{1,0:T(8,128)(2,1)}, u32[]{:S(2)}) copy-start(bf16[512,256]{1,0:T(8,128)(2,1)} %param.11) | copy-start | bytes 786436
  11.8 187.8 %reduce-scatter.2.cloned.1.call-start = ((), (), s32[]{:S(2)}) async-start(), calls=%async_computation.1 | async-start | bytes 4456448 | tf_op jit(solution)/shard_map/reduce_scatter | solution.py:62
  51.3 46.2 %copy-start.1 = (bf16[512,256]{1,0:T(8,128)(2,1)S(1)}, bf16[512,256]{1,0:T(8,128)(2,1)}, u32[]{:S(2)}) copy-start(bf16[512,256]{1,0:T(8,128)(2,1)} %param.9) | copy-start | bytes 786436
  52.8 45.2 %copy-start.3 = (f32[256]{0:T(256)S(1)}, f32[256]{0:T(256)}, u32[]{:S(2)}) copy-start(f32[256]{0:T(256)} %param.13) | copy-start | bytes 3076
  101.3 98.3 %copy-start.2 = (bf16[32,4096]{1,0:T(8,128)(2,1)S(1)}, bf16[32,4096]{1,0:T(8,128)(2,1)}, u32[]{:S(2)}) copy-start(bf16[32,4096]{1,0:T(8,128)(2,1)} %param.15) | copy-start | bytes 786436
Sparse Core Ops, SparseCore 0:
  12.0 85.4 all-gather.3
  101.5 98.0 reduce-scatter.1
where the time goes:
time: 211 us; the launch traced here: 208 us
  waiting for transfers between devices  143 us (68%)
  blocking collectives  37.6 us (18%)
  between operations  13.5 us (6%)
  matrix products  8.57 us (4%)
  other arithmetic  2.85 us (1%)
  local copies, waits for them, and re-layouts  2.65 us (1%)
    reduce_scatter x1, waiting for transfers between devices, shards(): lax.psum_scatter(jnp.dot(normed, out_weight, preferred_element_type=jnp.f...  98.3 us
    all_gather x1, waiting for transfers between devices, entering(): lax.all_gather(a.astype(kind), axis)  44.7 us
    all_gather x1, blocking collectives, entering(): lax.all_gather(a.astype(kind), axis)  37.6 us
  transfers between devices with their start and end apart: 2, of which 2 were waited for; matrix products, arithmetic and copies ran while one was open for 2% of the time, Pallas kernels for 0%

commit v1 on v0

v1 whole, which is shorter than its diff:
```python
import functools

import jax
import jax.numpy as jnp
from jax import lax
from jax.experimental import pallas as pl
from jax.experimental.pallas import tpu as pltpu
from jax.sharding import PartitionSpec as P

MESH = pl.DeviceIdType.MESH
F32, BF16 = jnp.float32, jnp.bfloat16
NZ = 8
HEADS, HD = 2, 128
SLICE = HD // NZ
BODY = HEADS * SLICE
MSG = BODY + 16
STREAMS = 8
NT = (((1,), (1,)), ((), ()))
TN = (((0,), (0,)), ((), ()))


def dot(a, b, dims=(((1,), (0,)), ((), ()))):
    return lax.dot_general(a, b, dims, preferred_element_type=F32)


def thirds(x):
    hi = x.astype(BF16).astype(F32)
    mid = (x - hi).astype(BF16).astype(F32)
    return hi, mid, x - hi - mid


def decay_tile(totals):
    row = lax.broadcasted_iota(jnp.int32, (16, HD), 0)
    tile = jnp.zeros((16, HD), F32)
    for h, total in enumerate(totals):
        for j, part in enumerate(thirds(total)):
            tile = jnp.where(row == 3 * h + j, part, tile)
    return tile.astype(BF16)


def read_decay(tile):
    t = tile.astype(F32)
    return [t[3 * h : 3 * h + 1] + t[3 * h + 1 : 3 * h + 2] + t[3 * h + 2 : 3 * h + 3] for h in range(HEADS)]


def per_head(pair):
    row = lax.broadcasted_iota(jnp.int32, (BODY, HD), 0)
    return jnp.where(row < SLICE, pair[0], pair[1])


def kernel(
    nx, ny,
    q_in, k_in, v_in, ld_in, gain_in, w_ref, res_ref, out_ref,
    q_ref, k_ref, v_ref, ld_ref, gain_ref, wbuf, resbuf, sbuf, abuf, xsend, xbuf, psend, pbuf, att, grown, nbuf, nrecv, part, rbuf,
    load_sem, core_send, core_recv, a_send, a_recv, x_send, x_recv, p_send, p_recv, ring_send, ring_recv,
):
    ctx, ex = lax.axis_index("ctx"), lax.axis_index("exp")
    x, z = ctx // NZ, lax.rem(ctx, NZ)
    y, core = ex // 2, lax.rem(ex, 2)
    rows = q_in.shape[0]
    kdim = w_ref.shape[0]
    mate = (ctx, y * 2 + 1 - core)
    up = (ctx, lax.rem(y + 1, ny) * 2 + core)
    down = (ctx, lax.rem(y + ny - 1, ny) * 2 + core)

    def z_peer(j):
        return lax.rem(z + j, NZ)

    def x_peer(j):
        return lax.rem(x + j, nx)

    loads = [
        pltpu.make_async_copy(a, b, load_sem.at[2 + i])
        for i, (a, b) in enumerate(
            ((ld_in, ld_ref), (k_in, k_ref), (v_in, v_ref), (q_in, q_ref), (gain_in, gain_ref))
        )
    ]
    for load in loads:
        load.start()
    load_w = pltpu.make_async_copy(w_ref, wbuf.at[pl.ds(0, kdim)], load_sem.at[0])
    load_w.start()
    load_res = pltpu.make_async_copy(res_ref, resbuf, load_sem.at[1])
    load_res.start()

    barrier = pltpu.get_barrier_semaphore()
    peers = [(x * NZ + z_peer(j), ex) for j in range(1, NZ)]
    peers += [(x_peer(j) * NZ + z, ex) for j in range(1, nx)]
    peers += [up, down, mate]
    for peer in peers:
        pl.semaphore_signal(barrier, inc=1, device_id=peer, device_id_type=MESH)

    loads[0].wait()
    ld = jnp.concatenate([ld_ref[...]] * (8 // HEADS), axis=0)
    hi, mid, lo = thirds(ld)
    kind = lax.broadcasted_iota(jnp.int32, ld.shape, 0) // HEADS
    parts = jnp.where(kind == 0, hi, jnp.where(kind == 1, mid, jnp.where(kind == 2, lo, 0.0))).astype(BF16)
    ti = lax.broadcasted_iota(jnp.int32, (rows, rows), 0)
    si = lax.broadcasted_iota(jnp.int32, (rows, rows), 1)
    tri = jnp.where(si <= ti, 1.0, 0.0).astype(BF16)
    by_col = dot(tri, parts, NT)
    by_row = dot(parts, tri, NT)
    cum_col = [by_col[:, h : h + 1] + by_col[:, 2 + h : 3 + h] + by_col[:, 4 + h : 5 + h] for h in range(HEADS)]
    cum_row = [by_row[h : h + 1] + by_row[2 + h : 3 + h] + by_row[4 + h : 5 + h] for h in range(HEADS)]
    total = [jnp.broadcast_to(c[rows - 1 : rows], (1, HD)) for c in cum_col]
    for h in range(HEADS):
        grown[:, h : h + 1] = jnp.exp(cum_col[h])

    tile = decay_tile(total)
    loads[1].wait()
    loads[2].wait()
    for h in range(HEADS):
        cols = slice(h * HD, (h + 1) * HD)
        keyed = (k_ref[:, cols].astype(F32) * jnp.exp(total[h] - cum_col[h])).astype(BF16)
        state = dot(keyed, v_ref[:, cols], TN)
        sbuf[:, h * SLICE : (h + 1) * SLICE, :] = state.astype(BF16).reshape(NZ, SLICE, HD)
    for j in range(NZ):
        sbuf[j, BODY:MSG, :] = tile

    pl.semaphore_wait(barrier, len(peers))

    def a_copy(j):
        return pltpu.make_async_remote_copy(
            sbuf.at[z_peer(j)], abuf.at[z], a_send.at[j], a_recv.at[j],
            device_id=(x * NZ + z_peer(j), ex), device_id_type=MESH,
        )

    def x_copy(j):
        return pltpu.make_async_remote_copy(
            xsend, xbuf.at[x], x_send.at[j], x_recv.at[j],
            device_id=(x_peer(j) * NZ + z, ex), device_id_type=MESH,
        )

    def p_copy(j):
        return pltpu.make_async_remote_copy(
            psend.at[z_peer(j)], pbuf.at[z], p_send.at[j], p_recv.at[j],
            device_id=(x * NZ + z_peer(j), ex), device_id_type=MESH,
        )

    for j in range(1, NZ):
        a_copy(j).start()
    w_copy = pltpu.make_async_remote_copy(
        w_ref, wbuf.at[pl.ds(kdim, kdim)], core_send.at[0], core_recv.at[0], device_id=mate, device_id_type=MESH
    )
    w_copy.start()
    abuf[z] = sbuf[z]

    def attend(h, i):
        cols = slice(h * HD, (h + 1) * HD)
        r0, end = i * HD, (i + 1) * HD
        scores = dot(q_ref[r0:end, cols], k_ref[:end, cols], NT)
        spread = cum_col[h][r0:end] - cum_row[h][:, :end]
        at = lax.broadcasted_iota(jnp.int32, (HD, end), 0) + r0
        seen = lax.broadcasted_iota(jnp.int32, (HD, end), 1) <= at
        weight = jnp.exp(jnp.where(seen, spread, -1e30))
        att[r0:end, cols] = dot((scores * weight).astype(BF16), v_ref[:end, cols])

    loads[3].wait()
    loads[4].wait()
    for i in range(rows // HD):
        attend(0, i)

    for j in range(1, NZ):
        a_copy(j).wait_recv()
    state = jnp.zeros((BODY, HD), F32)
    run = [jnp.zeros((1, HD), F32)] * HEADS
    inner, passed = [], []
    for j in range(NZ):
        inner.append(state)
        passed.append(run)
        own = read_decay(abuf[j, BODY:MSG, :])
        state = state * jnp.exp(per_head(own)) + abuf[j, :BODY, :].astype(F32)
        run = [a + b for a, b in zip(run, own)]
    xsend[:BODY, :] = state.astype(BF16)
    xsend[BODY:, :] = decay_tile(run)
    for j in range(1, nx):
        x_copy(j).start()
    xbuf[x] = xsend[...]

    for i in range(rows // HD - 1):
        attend(1, i)

    for j in range(1, nx):
        x_copy(j).wait_recv()
    base = jnp.zeros((BODY, HD), F32)
    for j in range(nx - 1):
        own = read_decay(xbuf[j, BODY:MSG, :])
        later = base * jnp.exp(per_head(own)) + xbuf[j, :BODY, :].astype(F32)
        base = jnp.where(j < x, later, base)
    for j in range(NZ):
        psend[j] = (inner[j] + base * jnp.exp(per_head(passed[j]))).astype(BF16)
    for j in range(1, NZ):
        p_copy(j).start()
    pbuf[z] = psend[z]

    attend(1, rows // HD - 1)

    for j in range(1, NZ):
        p_copy(j).wait_recv()

    far = ny // 2
    order = [far, far - 1, 1 - far]
    for r in range(far - 2, 0, -1):
        order += [r, -r]
    order.append(0)
    place = {r % ny: i for i, r in enumerate(order)}
    near = rows // ny
    mine = near // 2
    wide = part.shape[-1]
    state_in = [pbuf[:, h * SLICE : (h + 1) * SLICE, :].reshape(HD, HD) for h in range(HEADS)]

    def n_copy(g):
        p = pl.ds(groups[g][0], groups[g][1])
        return pltpu.make_async_remote_copy(
            nbuf.at[p, 1 - core], nrecv.at[p], core_send.at[1 + g], core_recv.at[1 + g],
            device_id=mate, device_id_type=MESH,
        )

    def norm(g):
        start, count = groups[g]
        at = [pl.ds(pl.multiple_of(lax.rem(y + r + ny, ny) * near, near), near) for r in order[start : start + count]]
        up_to = jnp.concatenate([grown[a] for a in at], axis=0)
        for h in range(HEADS):
            cols = slice(h * HD, (h + 1) * HD)
            query = jnp.concatenate([q_ref[a, cols] for a in at], axis=0)
            local = jnp.concatenate([att[a, cols] for a in at], axis=0)
            whole = local + dot(query, state_in[h]) * up_to[:, h : h + 1]
            mean = jnp.mean(whole * whole, axis=-1, keepdims=True)
            normed = whole * lax.rsqrt(mean + 1e-6) * gain_ref[:, cols]
            nbuf[start : start + count, :, :, cols] = normed.astype(BF16).reshape(count, 2, mine, HD)
        n_copy(g).start()

    def project(g, b, lhs):
        start, count = groups[g]
        c0 = column(b)
        part[b, start : start + count] = dot(lhs, wbuf[:, c0 : c0 + wide]).astype(BF16).reshape(count, mine, wide)

    def lhs_of(g):
        start, count = groups[g]
        n_copy(g).wait_recv()
        own = nbuf[start : start + count, core].reshape(count * mine, kdim)
        other = nrecv[start : start + count].reshape(count * mine, kdim)
        return jnp.concatenate([own, other], axis=1)

    def column(b):
        return ((b % 2) * (STREAMS // 2) + b // 2) * wide

    def hops(b, upward):
        return far if (b % 2 == 0) == upward else far - 1

    def owed(b, upward, hop):
        left = hops(b, upward) - hop
        return place[(left if upward else -left) % ny]

    def slot(b, upward, hop):
        return hop if upward else hops(b, True) + hop

    def chain(b, upward, hop):
        source = part.at[b, owed(b, upward, hop)] if hop == 0 else rbuf.at[b, slot(b, upward, hop - 1)]
        at = slot(b, upward, hop)
        return pltpu.make_async_remote_copy(
            source, rbuf.at[b, at], ring_send.at[b, at], ring_recv.at[b, at],
            device_id=up if upward else down, device_id_type=MESH,
        )

    groups = [(0, 3), (3, ny - 3)]
    norm(0)
    norm(1)
    load_w.wait()
    w_copy.wait_recv()
    lhs = lhs_of(0)
    for b in range(STREAMS):
        project(0, b, lhs)
        for upward in (True, False):
            chain(b, upward, 0).start()
    lhs = lhs_of(1)
    for b in range(STREAMS):
        project(1, b, lhs)

    for hop in range(1, far):
        for b in range(STREAMS):
            for upward in (True, False):
                if hop < hops(b, upward):
                    chain(b, upward, hop - 1).wait_recv()
                    at = slot(b, upward, hop - 1)
                    own = part[b, owed(b, upward, hop)].astype(F32)
                    rbuf[b, at] = (rbuf[b, at].astype(F32) + own).astype(BF16)
                    chain(b, upward, hop).start()

    load_res.wait()
    for b in range(STREAMS):
        c0 = column(b)
        summed = resbuf[:, c0 : c0 + wide].astype(F32) + part[b, place[0]].astype(F32)
        for upward in (True, False):
            last = hops(b, upward) - 1
            chain(b, upward, last).wait_recv()
            summed += rbuf[b, slot(b, upward, last)].astype(F32)
        out_ref[:, c0 : c0 + wide] = summed.astype(BF16)

    for j in range(1, NZ):
        a_copy(j).wait_send()
        p_copy(j).wait_send()
    for j in range(1, nx):
        x_copy(j).wait_send()
    w_copy.wait_send()
    for g in range(len(groups)):
        n_copy(g).wait_send()
    for b in range(STREAMS):
        for upward in (True, False):
            for hop in range(hops(b, upward)):
                chain(b, upward, hop).wait_send()


def solution(mesh):
    nx, ny = mesh.shape["ctx"] // NZ, mesh.shape["exp"] // 2

    def shards(q_spikes, k_spikes, v_spikes, log_decay, norm_gain, out_weight, residual):
        rows = q_spikes.shape[0]
        kdim, width = out_weight.shape
        mine = residual.shape[0]
        wide = width // STREAMS
        vmem = pl.BlockSpec(memory_space=pltpu.VMEM)
        hbm = pl.BlockSpec(memory_space=pltpu.HBM)
        dma = pltpu.SemaphoreType.DMA
        args = (q_spikes, k_spikes, v_spikes, log_decay.T, norm_gain.reshape(1, -1), out_weight, residual)
        return pl.pallas_call(
            functools.partial(kernel, nx, ny),
            out_shape=pltpu.VMEM(residual.shape, BF16),
            in_specs=[hbm] * 7,
            out_specs=vmem,
            scratch_shapes=[
                pltpu.VMEM(q_spikes.shape, BF16),
                pltpu.VMEM(q_spikes.shape, BF16),
                pltpu.VMEM(q_spikes.shape, BF16),
                pltpu.VMEM((HEADS, rows), F32),
                pltpu.VMEM((1, kdim), F32),
                pltpu.VMEM((2 * kdim, width), BF16),
                pltpu.VMEM((mine, width), BF16),
                pltpu.VMEM((NZ, MSG, HD), BF16),
                pltpu.VMEM((NZ, MSG, HD), BF16),
                pltpu.VMEM((MSG, HD), BF16),
                pltpu.VMEM((nx, MSG, HD), BF16),
                pltpu.VMEM((NZ, BODY, HD), BF16),
                pltpu.VMEM((NZ, BODY, HD), BF16),
                pltpu.VMEM((rows, HEADS * HD), F32),
                pltpu.VMEM((rows, HD), F32),
                pltpu.VMEM((ny, 2, mine, kdim), BF16),
                pltpu.VMEM((ny, mine, kdim), BF16),
                pltpu.VMEM((STREAMS, ny, mine, wide), BF16),
                pltpu.VMEM((STREAMS, ny - 1, mine, wide), BF16),
                dma((7,)), dma((3,)), dma((3,)), dma((NZ,)), dma((NZ,)), dma((nx,)), dma((nx,)),
                dma((NZ,)), dma((NZ,)), dma((STREAMS, ny - 1)), dma((STREAMS, ny - 1)),
            ],
            compiler_params=pltpu.CompilerParams(
                collective_id=0, has_side_effects=True, vmem_limit_bytes=48 * 2**20
            ),
        )(*[pltpu.with_memory_space_constraint(a, pltpu.HBM) for a in args])

    return jax.shard_map(
        shards,
        mesh=mesh,
        in_specs=(
            P("ctx", "exp"),
            P("ctx", "exp"),
            P("ctx", "exp"),
            P("ctx", "exp"),
            P("exp"),
            P("exp", None),
            P(("ctx", "exp"), None),
        ),
        out_specs=P(("ctx", "exp"), None),
        check_vma=False,
    )
```

time: 211 us -> 54.2 us (0.26); the launches traced: 208 us -> 54.1 us
  waiting for transfers between devices: 143 us -> 0 us
  Pallas kernels: 0 us -> 53.4 us
  blocking collectives: 37.6 us -> 0 us
  between operations: 13.5 us -> 0.01 us
  matrix products: 8.57 us -> 0 us
  other arithmetic: 2.85 us -> 0 us
    reduce_scatter x1 -> x0, waiting for transfers between devices: 98.3 us -> none  [shards(): lax.psum_scatter(jnp.dot(normed, out_weight, preferred_element_type=jnp.f...]
    pallas_call x0 -> x1, Pallas kernels: none -> 53.4 us  [shards(): pl.pallas_call(functools.partial(kernel, nx, ny), out_shape=pltpu.VMEM(re...]
    all_gather x1 -> x0, waiting for transfers between devices: 44.7 us -> none  [entering(): lax.all_gather(a.astype(kind), axis)]
    all_gather x1 -> x0, blocking collectives: 37.6 us -> none  [entering(): lax.all_gather(a.astype(kind), axis)]
    dot_general x5 -> x0, matrix products: 8.57 us -> none  [the longest x1 3.22 us: shards(): jnp.dot(normed, out_weight, preferred_element_type=jnp.float32)]
  transfers between devices with their start and end apart: 2 -> 0, of which waited for: 2 -> 0; matrix products, arithmetic and copies ran while one was open for 2% -> 0% of each run, Pallas kernels for 0% -> 0%
where the time goes in v1:
time: 54.2 us; the launch traced here: 54.1 us
  Pallas kernels  53.4 us (99%)
  local copies, waits for them, and re-layouts  0.71 us (1%)
    pallas_call x1, Pallas kernels, shards(): pl.pallas_call(functools.partial(kernel, nx, ny), out_shape=pltpu.VMEM(re...  53.4 us

profile of v1, /device:TPU:1, one launch (start us, length us, event | category | flops | bytes accessed | tf_op | source)
XLA Modules:
  0.0 54.1 jit_solution(6231013354952182972)
XLA Ops:
  0.0 53.4 %shard_map.73 = bf16[32,4096]{1,0:T(8,128)(2,1)S(1)} custom-call(bf16[512,256]{1,0:T(8,128)(2,1)} %q_in.1, bf16[512,256]{1,0:T(8,128)(2,1)} %k_in.1, bf16[512,256]{1,0:T(8,128)(2,1)} %v_in.1, f32[2,512]{1,0:T(2,128)} %bitcast.2, f32[1,256]{1,0:T(1,128)} %bitcast.3, bf16[256,4096]{1,0:T(8,128)(2,1)} %w_ref.1, bf16[32,4096]{1,0:T(8,128)(2,1)} %res_ref.1), custom_call_target="tpu_custom_call" | custom-call | tf_op jit(solution)/shard_map/pallas_call | solution.py:325
  53.4 0.7 %copy.9 = bf16[32,4096]{1,0:T(8,128)(2,1)} copy(bf16[32,4096]{1,0:T(8,128)(2,1)S(1)} %shard_map.73) | data formatting | bytes 524288

commit v2 on v1

--- a/solution.py
+++ b/solution.py
@@ -14,7 +14,7 @@
 SLICE = HD // NZ
 BODY = HEADS * SLICE
 MSG = BODY + 16
-STREAMS = 8
+STREAMS = 4
 NT = (((1,), (1,)), ((), ()))
 TN = (((0,), (0,)), ((), ()))
 
@@ -69,6 +69,13 @@
     def x_peer(j):
         return lax.rem(x + j, nx)
 
+    barrier = pltpu.get_barrier_semaphore()
+    peers = [(x * NZ + z_peer(j), ex) for j in sorted(range(1, NZ), key=lambda j: -min(j, NZ - j))]
+    peers += [(x_peer(j) * NZ + z, ex) for j in range(1, nx)]
+    peers += [up, down, mate]
+    for peer in peers:
+        pl.semaphore_signal(barrier, inc=1, device_id=peer, device_id_type=MESH)
+
     loads = [
         pltpu.make_async_copy(a, b, load_sem.at[2 + i])
         for i, (a, b) in enumerate(
@@ -81,13 +88,6 @@
     load_w.start()
     load_res = pltpu.make_async_copy(res_ref, resbuf, load_sem.at[1])
     load_res.start()
-
-    barrier = pltpu.get_barrier_semaphore()
-    peers = [(x * NZ + z_peer(j), ex) for j in range(1, NZ)]
-    peers += [(x_peer(j) * NZ + z, ex) for j in range(1, nx)]
-    peers += [up, down, mate]
-    for peer in peers:
-        pl.semaphore_signal(barrier, inc=1, device_id=peer, device_id_type=MESH)
 
     loads[0].wait()
     ld = jnp.concatenate([ld_ref[...]] * (8 // HEADS), axis=0)
@@ -232,7 +232,7 @@
     def project(g, b, lhs):
         start, count = groups[g]
         c0 = column(b)
-        part[b, start : start + count] = dot(lhs, wbuf[:, c0 : c0 + wide]).astype(BF16).reshape(count, mine, wide)
+        part[index(b), start : start + count] = dot(lhs, wbuf[:, pl.ds(c0, wide)]).astype(BF16).reshape(count, mine, wide)
 
     def lhs_of(g):
         start, count = groups[g]
@@ -242,10 +242,15 @@
         return jnp.concatenate([own, other], axis=1)
 
     def column(b):
-        return ((b % 2) * (STREAMS // 2) + b // 2) * wide
+        pair, half = b
+        c0 = half * (STREAMS // 2) * wide
+        return c0 + pair * wide if isinstance(pair, int) else pl.multiple_of(c0 + pair * wide, wide)
+
+    def index(b):
+        return b[0] * 2 + b[1]
 
     def hops(b, upward):
-        return far if (b % 2 == 0) == upward else far - 1
+        return far if (b[1] == 0) == upward else far - 1
 
     def owed(b, upward, hop):
         left = hops(b, upward) - hop
@@ -255,12 +260,20 @@
         return hop if upward else hops(b, True) + hop
 
     def chain(b, upward, hop):
-        source = part.at[b, owed(b, upward, hop)] if hop == 0 else rbuf.at[b, slot(b, upward, hop - 1)]
+        source = part.at[index(b), owed(b, upward, hop)] if hop == 0 else rbuf.at[index(b), slot(b, upward, hop - 1)]
         at = slot(b, upward, hop)
         return pltpu.make_async_remote_copy(
-            source, rbuf.at[b, at], ring_send.at[b, at], ring_recv.at[b, at],
+            source, rbuf.at[index(b), at], ring_send.at[index(b), at], ring_recv.at[index(b), at],
             device_id=up if upward else down, device_id_type=MESH,
         )
+
+    def each(body):
+        def step(pair, carry):
+            for half in (0, 1):
+                body((pair, half))
+            return carry
+
+        lax.fori_loop(0, STREAMS // 2, step, 0)
 
     groups = [(0, 3), (3, ny - 3)]
     norm(0)
@@ -268,33 +281,41 @@
     load_w.wait()
     w_copy.wait_recv()
     lhs = lhs_of(0)
-    for b in range(STREAMS):
+
+    def first(b):
         project(0, b, lhs)
         for upward in (True, False):
             chain(b, upward, 0).start()
-    lhs = lhs_of(1)
-    for b in range(STREAMS):
-        project(1, b, lhs)
+
+    each(first)
+    rest = lhs_of(1)
+    each(lambda b: project(1, b, rest))
 
     for hop in range(1, far):
-        for b in range(STREAMS):
+
+        def pass_on(b, hop=hop):
             for upward in (True, False):
                 if hop < hops(b, upward):
                     chain(b, upward, hop - 1).wait_recv()
                     at = slot(b, upward, hop - 1)
-                    own = part[b, owed(b, upward, hop)].astype(F32)
-                    rbuf[b, at] = (rbuf[b, at].astype(F32) + own).astype(BF16)
+                    own = part[index(b), owed(b, upward, hop)].astype(F32)
+                    rbuf[index(b), at] = (rbuf[index(b), at].astype(F32) + own).astype(BF16)
                     chain(b, upward, hop).start()
 
+        each(pass_on)
+
     load_res.wait()
-    for b in range(STREAMS):
-        c0 = column(b)
-        summed = resbuf[:, c0 : c0 + wide].astype(F32) + part[b, place[0]].astype(F32)
+
+    def finish(b):
+        at = pl.ds(column(b), wide)
+        summed = resbuf[:, at].astype(F32) + part[index(b), place[0]].astype(F32)
         for upward in (True, False):
             last = hops(b, upward) - 1
             chain(b, upward, last).wait_recv()
-            summed += rbuf[b, slot(b, upward, last)].astype(F32)
-        out_ref[:, c0 : c0 + wide] = summed.astype(BF16)
+            summed += rbuf[index(b), slot(b, upward, last)].astype(F32)
+        out_ref[:, at] = summed.astype(BF16)
+
+    each(finish)
 
     for j in range(1, NZ):
         a_copy(j).wait_send()
@@ -304,10 +325,13 @@
     w_copy.wait_send()
     for g in range(len(groups)):
         n_copy(g).wait_send()
-    for b in range(STREAMS):
+
+    def drain(b):
         for upward in (True, False):
             for hop in range(hops(b, upward)):
                 chain(b, upward, hop).wait_send()
+
+    each(drain)
 
 
 def solution(mesh):

time: 54.2 us -> 53.8 us (level)
  no operation moved by 1% of the time
where the time goes in v2:
time: 53.8 us; the launch traced here: 53.7 us
  Pallas kernels  53 us (99%)
  local copies, waits for them, and re-layouts  0.71 us (1%)
    pallas_call x1, Pallas kernels, shards(): pl.pallas_call(functools.partial(kernel, nx, ny), out_shape=pltpu.VMEM(re...  53 us

profile of v2, /device:TPU:1, one launch (start us, length us, event | category | flops | bytes accessed | tf_op | source)
XLA Modules:
  0.0 53.7 jit_solution(2221144462875820709)
XLA Ops:
  0.0 53.0 %shard_map.73 = bf16[32,4096]{1,0:T(8,128)(2,1)S(1)} custom-call(bf16[512,256]{1,0:T(8,128)(2,1)} %q_in.1, bf16[512,256]{1,0:T(8,128)(2,1)} %k_in.1, bf16[512,256]{1,0:T(8,128)(2,1)} %v_in.1, f32[2,512]{1,0:T(2,128)} %bitcast.2, f32[1,256]{1,0:T(1,128)} %bitcast.3, bf16[256,4096]{1,0:T(8,128)(2,1)} %w_ref.1, bf16[32,4096]{1,0:T(8,128)(2,1)} %res_ref.1), custom_call_target="tpu_custom_call" | custom-call | tf_op jit(solution)/shard_map/pallas_call | solution.py:349
  53.0 0.7 %copy.9 = bf16[32,4096]{1,0:T(8,128)(2,1)} copy(bf16[32,4096]{1,0:T(8,128)(2,1)S(1)} %shard_map.73) | data formatting | bytes 524288

commit v3 on v2

--- a/solution.py
+++ b/solution.py
@@ -14,6 +14,7 @@
 SLICE = HD // NZ
 BODY = HEADS * SLICE
 MSG = BODY + 16
+EARLY = 2
 STREAMS = 4
 NT = (((1,), (1,)), ((), ()))
 TN = (((0,), (0,)), ((), ()))
@@ -51,8 +52,8 @@
 def kernel(
     nx, ny,
     q_in, k_in, v_in, ld_in, gain_in, w_ref, res_ref, out_ref,
-    q_ref, k_ref, v_ref, ld_ref, gain_ref, wbuf, resbuf, sbuf, abuf, xsend, xbuf, psend, pbuf, att, grown, nbuf, nrecv, part, rbuf,
-    load_sem, core_send, core_recv, a_send, a_recv, x_send, x_recv, p_send, p_recv, ring_send, ring_recv,
+    q_ref, k_ref, v_ref, ld_ref, gain_ref, wbuf, resbuf, sbuf, abuf, xsend, xbuf, psend, pbuf, direct, entering, att, grown, nbuf, nrecv, part, rbuf,
+    load_sem, core_send, core_recv, a_send, a_recv, x_send, x_recv, p_send, p_recv, r_send, r_recv, ring_send, ring_recv,
 ):
     ctx, ex = lax.axis_index("ctx"), lax.axis_index("exp")
     x, z = ctx // NZ, lax.rem(ctx, NZ)
@@ -75,6 +76,22 @@
     peers += [up, down, mate]
     for peer in peers:
         pl.semaphore_signal(barrier, inc=1, device_id=peer, device_id_type=MESH)
+
+    early = z < EARLY
+
+    def greet(c, carry):
+        @pl.when(lax.rem(c, NZ) != z)
+        def _():
+            pl.semaphore_signal(barrier, inc=1, device_id=(c, ex), device_id_type=MESH)
+
+        return carry
+
+    @pl.when(early)
+    def _():
+        lax.fori_loop(0, x * NZ, greet, 0)
+
+    directs = (nx - 1 - x) * EARLY
+    greeted = (nx - 1 - x) * (EARLY - early.astype(jnp.int32))
 
     loads = [
         pltpu.make_async_copy(a, b, load_sem.at[2 + i])
@@ -116,7 +133,7 @@
     for j in range(NZ):
         sbuf[j, BODY:MSG, :] = tile
 
-    pl.semaphore_wait(barrier, len(peers))
+    pl.semaphore_wait(barrier, len(peers) + greeted)
 
     def a_copy(j):
         return pltpu.make_async_remote_copy(
@@ -130,11 +147,39 @@
             device_id=(x_peer(j) * NZ + z, ex), device_id_type=MESH,
         )
 
-    def p_copy(j):
-        return pltpu.make_async_remote_copy(
-            psend.at[z_peer(j)], pbuf.at[z], p_send.at[j], p_recv.at[j],
-            device_id=(x * NZ + z_peer(j), ex), device_id_type=MESH,
-        )
+    def p_copy(to):
+        return pltpu.make_async_remote_copy(
+            psend.at[to], pbuf.at[z], p_send.at[to], p_recv.at[z],
+            device_id=(x * NZ + to, ex), device_id_type=MESH,
+        )
+
+    def p_wait(source):
+        pltpu.make_async_remote_copy(
+            psend.at[source], pbuf.at[source], p_send.at[source], p_recv.at[source],
+            device_id=(x * NZ + source, ex), device_id_type=MESH,
+        ).wait_recv()
+
+    def others(indices, body):
+        for i in indices:
+            pl.when(z != i)(functools.partial(body, i))
+
+    def r_copy(t):
+        to = (x + 1 + t // EARLY) * NZ + lax.rem(t, EARLY)
+        return pltpu.make_async_remote_copy(
+            xsend, direct.at[ctx], r_send.at[t], r_recv.at[ctx], device_id=(to, ex), device_id_type=MESH
+        )
+
+    def r_wait(c):
+        pltpu.make_async_remote_copy(
+            xsend, direct.at[c], r_send.at[0], r_recv.at[c], device_id=(c, ex), device_id_type=MESH
+        ).wait_recv()
+
+    def count(body):
+        def step(i, carry):
+            body(i)
+            return carry
+
+        return step
 
     for j in range(1, NZ):
         a_copy(j).start()
@@ -163,15 +208,20 @@
         a_copy(j).wait_recv()
     state = jnp.zeros((BODY, HD), F32)
     run = [jnp.zeros((1, HD), F32)] * HEADS
-    inner, passed = [], []
+    inner, passed, row_decay = [], [], []
     for j in range(NZ):
         inner.append(state)
         passed.append(run)
         own = read_decay(abuf[j, BODY:MSG, :])
+        row_decay.append(own)
         state = state * jnp.exp(per_head(own)) + abuf[j, :BODY, :].astype(F32)
         run = [a + b for a, b in zip(run, own)]
     xsend[:BODY, :] = state.astype(BF16)
     xsend[BODY:, :] = decay_tile(run)
+    lax.fori_loop(0, directs, count(lambda t: r_copy(t).start()), 0)
+    for j in range(EARLY):
+        psend[j] = inner[j].astype(BF16)
+    others(range(EARLY), lambda i: p_copy(i).start())
     for j in range(1, nx):
         x_copy(j).start()
     xbuf[x] = xsend[...]
@@ -186,16 +236,30 @@
         own = read_decay(xbuf[j, BODY:MSG, :])
         later = base * jnp.exp(per_head(own)) + xbuf[j, :BODY, :].astype(F32)
         base = jnp.where(j < x, later, base)
-    for j in range(NZ):
+    for j in range(EARLY, NZ):
         psend[j] = (inner[j] + base * jnp.exp(per_head(passed[j]))).astype(BF16)
-    for j in range(1, NZ):
-        p_copy(j).start()
+    others(range(EARLY, NZ), lambda i: p_copy(i).start())
     pbuf[z] = psend[z]
 
     attend(1, rows // HD - 1)
 
-    for j in range(1, NZ):
-        p_copy(j).wait_recv()
+    others(range(NZ), p_wait)
+
+    @pl.when(early)
+    def _():
+        lax.fori_loop(0, x * NZ, count(r_wait), 0)
+        since = per_head([sum(jnp.where(j < z, own[h], 0.0) for j, own in enumerate(row_decay)) for h in range(HEADS)])
+        entering[...] = jnp.zeros_like(entering)
+
+        def join(row):
+            own = jnp.exp(per_head(read_decay(direct[row * NZ, BODY:MSG, :])))
+            for j in range(NZ):
+                entering[j] = entering[j] * own + direct[row * NZ + j, :BODY, :].astype(F32)
+
+        lax.fori_loop(0, x, count(join), 0)
+        factor = jnp.exp(since)
+        for j in range(NZ):
+            pbuf[j] = (pbuf[j].astype(F32) + entering[j] * factor).astype(BF16)
 
     far = ny // 2
     order = [far, far - 1, 1 - far]
@@ -319,7 +383,8 @@
 
     for j in range(1, NZ):
         a_copy(j).wait_send()
-        p_copy(j).wait_send()
+    others(range(NZ), lambda i: p_copy(i).wait_send())
+    lax.fori_loop(0, directs, count(lambda t: r_copy(t).wait_send()), 0)
     for j in range(1, nx):
         x_copy(j).wait_send()
     w_copy.wait_send()
@@ -365,6 +430,8 @@
                 pltpu.VMEM((nx, MSG, HD), BF16),
                 pltpu.VMEM((NZ, BODY, HD), BF16),
                 pltpu.VMEM((NZ, BODY, HD), BF16),
+                pltpu.VMEM(((nx - 1) * NZ, MSG, HD), BF16),
+                pltpu.VMEM((NZ, BODY, HD), F32),
                 pltpu.VMEM((rows, HEADS * HD), F32),
                 pltpu.VMEM((rows, HD), F32),
                 pltpu.VMEM((ny, 2, mine, kdim), BF16),
@@ -372,7 +439,7 @@
                 pltpu.VMEM((STREAMS, ny, mine, wide), BF16),
                 pltpu.VMEM((STREAMS, ny - 1, mine, wide), BF16),
                 dma((7,)), dma((3,)), dma((3,)), dma((NZ,)), dma((NZ,)), dma((nx,)), dma((nx,)),
-                dma((NZ,)), dma((NZ,)), dma((STREAMS, ny - 1)), dma((STREAMS, ny - 1)),
+                dma((NZ,)), dma((NZ,)), dma(((nx - 1) * EARLY,)), dma(((nx - 1) * NZ,)), dma((STREAMS, ny - 1)), dma((STREAMS, ny - 1)),
             ],
             compiler_params=pltpu.CompilerParams(
                 collective_id=0, has_side_effects=True, vmem_limit_bytes=48 * 2**20

time: 53.8 us -> 52.2 us (0.970)
  Pallas kernels: 53 us -> 51.3 us
    pallas_call x1, Pallas kernels: 53 us -> 51.3 us  [shards(): pl.pallas_call(functools.partial(kernel, nx, ny), out_shape=pltpu.VMEM(re...]
where the time goes in v3:
time: 52.2 us; the launch traced here: 52.1 us
  Pallas kernels  51.3 us (98%)
  local copies, waits for them, and re-layouts  0.71 us (1%)
    pallas_call x1, Pallas kernels, shards(): pl.pallas_call(functools.partial(kernel, nx, ny), out_shape=pltpu.VMEM(re...  51.3 us

profile of v3, /device:TPU:1, one launch (start us, length us, event | category | flops | bytes accessed | tf_op | source)
XLA Modules:
  0.0 52.1 jit_solution(17588803569068127416)
XLA Ops:
  0.0 51.3 %shard_map.73 = bf16[32,4096]{1,0:T(8,128)(2,1)S(1)} custom-call(bf16[512,256]{1,0:T(8,128)(2,1)} %q_in.1, bf16[512,256]{1,0:T(8,128)(2,1)} %k_in.1, bf16[512,256]{1,0:T(8,128)(2,1)} %v_in.1, f32[2,512]{1,0:T(2,128)} %bitcast.2, f32[1,256]{1,0:T(1,128)} %bitcast.3, bf16[256,4096]{1,0:T(8,128)(2,1)} %w_ref.1, bf16[32,4096]{1,0:T(8,128)(2,1)} %res_ref.1), custom_call_target="tpu_custom_call" | custom-call | tf_op jit(solution)/shard_map/pallas_call | solution.py:414
  51.4 0.7 %copy.9 = bf16[32,4096]{1,0:T(8,128)(2,1)} copy(bf16[32,4096]{1,0:T(8,128)(2,1)S(1)} %shard_map.73) | data formatting | bytes 524288

commit v4 on v3

--- a/solution.py
+++ b/solution.py
@@ -16,6 +16,7 @@
 MSG = BODY + 16
 EARLY = 2
 STREAMS = 4
+ABSORB = 1
 NT = (((1,), (1,)), ((), ()))
 TN = (((0,), (0,)), ((), ()))
 
@@ -52,8 +53,8 @@
 def kernel(
     nx, ny,
     q_in, k_in, v_in, ld_in, gain_in, w_ref, res_ref, out_ref,
-    q_ref, k_ref, v_ref, ld_ref, gain_ref, wbuf, resbuf, sbuf, abuf, xsend, xbuf, psend, pbuf, direct, entering, att, grown, nbuf, nrecv, part, rbuf,
-    load_sem, core_send, core_recv, a_send, a_recv, x_send, x_recv, p_send, p_recv, r_send, r_recv, ring_send, ring_recv,
+    q_ref, k_ref, v_ref, ld_ref, gain_ref, wbuf, resbuf, sbuf, abuf, xsend, xbuf, psend, pbuf, direct, entering, att, grown, nbuf, nrecv, wnext, head, part, rbuf,
+    load_sem, core_send, core_recv, a_send, a_recv, x_send, x_recv, p_send, p_recv, r_send, r_recv, y_send, y_recv, f_send, f_recv, h_send, h_recv, ring_send, ring_recv,
 ):
     ctx, ex = lax.axis_index("ctx"), lax.axis_index("exp")
     x, z = ctx // NZ, lax.rem(ctx, NZ)
@@ -64,6 +65,8 @@
     up = (ctx, lax.rem(y + 1, ny) * 2 + core)
     down = (ctx, lax.rem(y + ny - 1, ny) * 2 + core)
 
+    aslant = [(ctx, lax.rem(y + d, ny) * 2 + 1 - core) for d in (1, ny - 1)]
+
     def z_peer(j):
         return lax.rem(z + j, NZ)
 
@@ -73,7 +76,7 @@
     barrier = pltpu.get_barrier_semaphore()
     peers = [(x * NZ + z_peer(j), ex) for j in sorted(range(1, NZ), key=lambda j: -min(j, NZ - j))]
     peers += [(x_peer(j) * NZ + z, ex) for j in range(1, nx)]
-    peers += [up, down, mate]
+    peers += [up, down, mate, *aslant]
     for peer in peers:
         pl.semaphore_signal(barrier, inc=1, device_id=peer, device_id_type=MESH)
 
@@ -187,6 +190,31 @@
         w_ref, wbuf.at[pl.ds(kdim, kdim)], core_send.at[0], core_recv.at[0], device_id=mate, device_id_type=MESH
     )
     w_copy.start()
+    half_cols = w_ref.shape[1] // 2
+    block = half_cols // (STREAMS // 2)
+
+    def y_copy(d, p):
+        there = wnext.at[d, pl.ds(0, kdim), pl.ds(p * block, block)]
+        return pltpu.make_async_remote_copy(
+            w_ref.at[:, pl.ds(d * half_cols + p * block, block)], there, y_send.at[d, p], y_recv.at[d, p],
+            device_id=(up, down)[d], device_id_type=MESH,
+        )
+
+    def f_copy(d, p):
+        cols = pl.ds(p * block, block)
+        return pltpu.make_async_remote_copy(
+            wnext.at[d, pl.ds(0, kdim), cols], wnext.at[d, pl.ds(kdim, kdim), cols], f_send.at[d, p], f_recv.at[d, p],
+            device_id=mate, device_id_type=MESH,
+        )
+
+    def hand_on(p):
+        for d in (0, 1):
+            y_copy(d, p).wait_recv()
+            f_copy(d, p).start()
+
+    for p in range(ABSORB):
+        for d in (0, 1):
+            y_copy(d, p).start()
     abuf[z] = sbuf[z]
 
     def attend(h, i):
@@ -293,6 +321,12 @@
             nbuf[start : start + count, :, :, cols] = normed.astype(BF16).reshape(count, 2, mine, HD)
         n_copy(g).start()
 
+    def h_copy(d, k):
+        return pltpu.make_async_remote_copy(
+            nbuf.at[0, lax.rem(core + k, 2)], head.at[d, k], h_send.at[d, k], h_recv.at[d, k],
+            device_id=(up, down)[d] if k == 0 else aslant[d], device_id_type=MESH,
+        )
+
     def project(g, b, lhs):
         start, count = groups[g]
         c0 = column(b)
@@ -331,42 +365,66 @@
             device_id=up if upward else down, device_id_type=MESH,
         )
 
-    def each(body):
+    def each(body, start=0, end=STREAMS // 2):
         def step(pair, carry):
             for half in (0, 1):
                 body((pair, half))
             return carry
 
-        lax.fori_loop(0, STREAMS // 2, step, 0)
+        lax.fori_loop(start, end, step, 0)
 
     groups = [(0, 3), (3, ny - 3)]
+    for p in range(ABSORB - 1):
+        hand_on(p)
     norm(0)
+    for d in (0, 1):
+        for k in (0, 1):
+            h_copy(d, k).start()
     norm(1)
     load_w.wait()
     w_copy.wait_recv()
     lhs = lhs_of(0)
 
-    def first(b):
+    def longer(b):
+        return b[1] == 0
+
+    def first(b, absorbed):
         project(0, b, lhs)
         for upward in (True, False):
-            chain(b, upward, 0).start()
-
-    each(first)
+            if not (absorbed and upward == longer(b)):
+                chain(b, upward, 0).start()
+
+    each(functools.partial(first, absorbed=True), 0, ABSORB)
+    each(functools.partial(first, absorbed=False), ABSORB)
+    hand_on(ABSORB - 1)
     rest = lhs_of(1)
+    for d in (0, 1):
+        for k in (0, 1):
+            h_copy(d, k).wait_recv()
+    heads = [jnp.concatenate([head[d, 0], head[d, 1]], axis=1) for d in (0, 1)]
+
+    for p in range(ABSORB):
+        for d in (0, 1):
+            b, upward = (p, d), d == 0
+            f_copy(d, p).wait_recv()
+            theirs = dot(heads[d], wnext[d, :, p * block : (p + 1) * block])
+            own = part[index(b), owed(b, upward, 1)].astype(F32)
+            rbuf[index(b), slot(b, upward, 0)] = (theirs + own).astype(BF16)
+            chain(b, upward, 1).start()
     each(lambda b: project(1, b, rest))
 
+    def pass_on(b, hop, absorbed):
+        for upward in (True, False):
+            if hop < hops(b, upward) and not (absorbed and hop == 1 and upward == longer(b)):
+                chain(b, upward, hop - 1).wait_recv()
+                at = slot(b, upward, hop - 1)
+                own = part[index(b), owed(b, upward, hop)].astype(F32)
+                rbuf[index(b), at] = (rbuf[index(b), at].astype(F32) + own).astype(BF16)
+                chain(b, upward, hop).start()
+
     for hop in range(1, far):
-
-        def pass_on(b, hop=hop):
-            for upward in (True, False):
-                if hop < hops(b, upward):
-                    chain(b, upward, hop - 1).wait_recv()
-                    at = slot(b, upward, hop - 1)
-                    own = part[index(b), owed(b, upward, hop)].astype(F32)
-                    rbuf[index(b), at] = (rbuf[index(b), at].astype(F32) + own).astype(BF16)
-                    chain(b, upward, hop).start()
-
-        each(pass_on)
+        each(functools.partial(pass_on, hop=hop, absorbed=True), 0, ABSORB)
+        each(functools.partial(pass_on, hop=hop, absorbed=False), ABSORB)
 
     load_res.wait()
 
@@ -391,12 +449,21 @@
     for g in range(len(groups)):
         n_copy(g).wait_send()
 
-    def drain(b):
+    for d in (0, 1):
+        for p in range(ABSORB):
+            y_copy(d, p).wait_send()
+            f_copy(d, p).wait_send()
+        for k in (0, 1):
+            h_copy(d, k).wait_send()
+
+    def drain(b, absorbed):
         for upward in (True, False):
             for hop in range(hops(b, upward)):
-                chain(b, upward, hop).wait_send()
-
-    each(drain)
+                if not (absorbed and hop == 0 and upward == longer(b)):
+                    chain(b, upward, hop).wait_send()
+
+    each(functools.partial(drain, absorbed=True), 0, ABSORB)
+    each(functools.partial(drain, absorbed=False), ABSORB)
 
 
 def solution(mesh):
@@ -436,10 +503,13 @@
                 pltpu.VMEM((rows, HD), F32),
                 pltpu.VMEM((ny, 2, mine, kdim), BF16),
                 pltpu.VMEM((ny, mine, kdim), BF16),
+                pltpu.VMEM((2, 2 * kdim, ABSORB * wide), BF16),
+                pltpu.VMEM((2, 2, mine, kdim), BF16),
                 pltpu.VMEM((STREAMS, ny, mine, wide), BF16),
                 pltpu.VMEM((STREAMS, ny - 1, mine, wide), BF16),
                 dma((7,)), dma((3,)), dma((3,)), dma((NZ,)), dma((NZ,)), dma((nx,)), dma((nx,)),
-                dma((NZ,)), dma((NZ,)), dma(((nx - 1) * EARLY,)), dma(((nx - 1) * NZ,)), dma((STREAMS, ny - 1)), dma((STREAMS, ny - 1)),
+                dma((NZ,)), dma((NZ,)), dma(((nx - 1) * EARLY,)), dma(((nx - 1) * NZ,)), dma((2, ABSORB)), dma((2, ABSORB)), dma((2, ABSORB)), dma((2, ABSORB)), dma((2, 2)), dma((2, 2)),
+                dma((STREAMS, ny - 1)), dma((STREAMS, ny - 1)),
             ],
             compiler_params=pltpu.CompilerParams(
                 collective_id=0, has_side_effects=True, vmem_limit_bytes=48 * 2**20

time: 52.2 us -> 51.3 us (0.983)
  Pallas kernels: 51.3 us -> 50.4 us
    pallas_call x1, Pallas kernels: 51.3 us -> 50.4 us  [shards(): pl.pallas_call(functools.partial(kernel, nx, ny), out_shape=pltpu.VMEM(re...]
where the time goes in v4:
time: 51.3 us; the launch traced here: 51.2 us
  Pallas kernels  50.4 us (98%)
  local copies, waits for them, and re-layouts  0.71 us (1%)
    pallas_call x1, Pallas kernels, shards(): pl.pallas_call(functools.partial(kernel, nx, ny), out_shape=pltpu.VMEM(re...  50.4 us

profile of v4, /device:TPU:1, one launch (start us, length us, event | category | flops | bytes accessed | tf_op | source)
XLA Modules:
  0.0 51.2 jit_solution(12164173305162668094)
XLA Ops:
  0.0 50.4 %shard_map.73 = bf16[32,4096]{1,0:T(8,128)(2,1)S(1)} custom-call(bf16[512,256]{1,0:T(8,128)(2,1)} %q_in.1, bf16[512,256]{1,0:T(8,128)(2,1)} %k_in.1, bf16[512,256]{1,0:T(8,128)(2,1)} %v_in.1, f32[2,512]{1,0:T(2,128)} %bitcast.2, f32[1,256]{1,0:T(1,128)} %bitcast.3, bf16[256,4096]{1,0:T(8,128)(2,1)} %w_ref.1, bf16[32,4096]{1,0:T(8,128)(2,1)} %res_ref.1), custom_call_target="tpu_custom_call" | custom-call | tf_op jit(solution)/shard_map/pallas_call | solution.py:481
  50.5 0.7 %copy.9 = bf16[32,4096]{1,0:T(8,128)(2,1)} copy(bf16[32,4096]{1,0:T(8,128)(2,1)S(1)} %shard_map.73) | data formatting | bytes 524288

commit v5 on v4

--- a/solution.py
+++ b/solution.py
@@ -53,7 +53,7 @@
 def kernel(
     nx, ny,
     q_in, k_in, v_in, ld_in, gain_in, w_ref, res_ref, out_ref,
-    q_ref, k_ref, v_ref, ld_ref, gain_ref, wbuf, resbuf, sbuf, abuf, xsend, xbuf, psend, pbuf, direct, entering, att, grown, nbuf, nrecv, wnext, head, part, rbuf,
+    q_ref, kv_ref, ld_ref, gain_ref, wbuf, resbuf, sbuf, abuf, xsend, xbuf, psend, pbuf, direct, entering, att, grown, nbuf, nrecv, wnext, head, part, rbuf,
     load_sem, core_send, core_recv, a_send, a_recv, x_send, x_recv, p_send, p_recv, r_send, r_recv, y_send, y_recv, f_send, f_recv, h_send, h_recv, ring_send, ring_recv,
 ):
     ctx, ex = lax.axis_index("ctx"), lax.axis_index("exp")
@@ -67,6 +67,9 @@
 
     aslant = [(ctx, lax.rem(y + d, ny) * 2 + 1 - core) for d in (1, ny - 1)]
 
+    def await_all(like, sem):
+        pltpu.make_async_copy(like, like, sem).wait()
+
     def z_peer(j):
         return lax.rem(z + j, NZ)
 
@@ -96,10 +99,11 @@
     directs = (nx - 1 - x) * EARLY
     greeted = (nx - 1 - x) * (EARLY - early.astype(jnp.int32))
 
+    k_ref, v_ref = kv_ref.at[0], kv_ref.at[1]
     loads = [
-        pltpu.make_async_copy(a, b, load_sem.at[2 + i])
-        for i, (a, b) in enumerate(
-            ((ld_in, ld_ref), (k_in, k_ref), (v_in, v_ref), (q_in, q_ref), (gain_in, gain_ref))
+        pltpu.make_async_copy(a, b, load_sem.at[i])
+        for a, b, i in (
+            (ld_in, ld_ref, 2), (k_in, k_ref, 3), (v_in, v_ref, 3), (q_in, q_ref, 4), (gain_in, gain_ref, 5)
         )
     ]
     for load in loads:
@@ -126,8 +130,7 @@
         grown[:, h : h + 1] = jnp.exp(cum_col[h])
 
     tile = decay_tile(total)
-    loads[1].wait()
-    loads[2].wait()
+    await_all(kv_ref, load_sem.at[3])
     for h in range(HEADS):
         cols = slice(h * HD, (h + 1) * HD)
         keyed = (k_ref[:, cols].astype(F32) * jnp.exp(total[h] - cum_col[h])).astype(BF16)
@@ -140,27 +143,21 @@
 
     def a_copy(j):
         return pltpu.make_async_remote_copy(
-            sbuf.at[z_peer(j)], abuf.at[z], a_send.at[j], a_recv.at[j],
+            sbuf.at[z_peer(j)], abuf.at[z], a_send, a_recv,
             device_id=(x * NZ + z_peer(j), ex), device_id_type=MESH,
         )
 
     def x_copy(j):
         return pltpu.make_async_remote_copy(
-            xsend, xbuf.at[x], x_send.at[j], x_recv.at[j],
+            xsend, xbuf.at[x], x_send, x_recv,
             device_id=(x_peer(j) * NZ + z, ex), device_id_type=MESH,
         )
 
     def p_copy(to):
         return pltpu.make_async_remote_copy(
-            psend.at[to], pbuf.at[z], p_send.at[to], p_recv.at[z],
+            psend.at[to], pbuf.at[z], p_send, p_recv,
             device_id=(x * NZ + to, ex), device_id_type=MESH,
         )
-
-    def p_wait(source):
-        pltpu.make_async_remote_copy(
-            psend.at[source], pbuf.at[source], p_send.at[source], p_recv.at[source],
-            device_id=(x * NZ + source, ex), device_id_type=MESH,
-        ).wait_recv()
 
     def others(indices, body):
         for i in indices:
@@ -169,13 +166,8 @@
     def r_copy(t):
         to = (x + 1 + t // EARLY) * NZ + lax.rem(t, EARLY)
         return pltpu.make_async_remote_copy(
-            xsend, direct.at[ctx], r_send.at[t], r_recv.at[ctx], device_id=(to, ex), device_id_type=MESH
-        )
-
-    def r_wait(c):
-        pltpu.make_async_remote_copy(
-            xsend, direct.at[c], r_send.at[0], r_recv.at[c], device_id=(c, ex), device_id_type=MESH
-        ).wait_recv()
+            xsend, direct.at[ctx], r_send.at[t // EARLY], r_recv.at[x], device_id=(to, ex), device_id_type=MESH
+        )
 
     def count(body):
         def step(i, carry):
@@ -196,21 +188,22 @@
     def y_copy(d, p):
         there = wnext.at[d, pl.ds(0, kdim), pl.ds(p * block, block)]
         return pltpu.make_async_remote_copy(
-            w_ref.at[:, pl.ds(d * half_cols + p * block, block)], there, y_send.at[d, p], y_recv.at[d, p],
+            w_ref.at[:, pl.ds(d * half_cols + p * block, block)], there, y_send, y_recv,
             device_id=(up, down)[d], device_id_type=MESH,
         )
 
     def f_copy(d, p):
         cols = pl.ds(p * block, block)
         return pltpu.make_async_remote_copy(
-            wnext.at[d, pl.ds(0, kdim), cols], wnext.at[d, pl.ds(kdim, kdim), cols], f_send.at[d, p], f_recv.at[d, p],
+            wnext.at[d, pl.ds(0, kdim), cols], wnext.at[d, pl.ds(kdim, kdim), cols], f_send, f_recv,
             device_id=mate, device_id_type=MESH,
         )
 
-    def hand_on(p):
-        for d in (0, 1):
-            y_copy(d, p).wait_recv()
-            f_copy(d, p).start()
+    def hand_on():
+        await_all(wnext.at[:, pl.ds(0, kdim)], y_recv)
+        for p in range(ABSORB):
+            for d in (0, 1):
+                f_copy(d, p).start()
 
     for p in range(ABSORB):
         for d in (0, 1):
@@ -232,8 +225,7 @@
     for i in range(rows // HD):
         attend(0, i)
 
-    for j in range(1, NZ):
-        a_copy(j).wait_recv()
+    await_all(abuf.at[pl.ds(0, NZ - 1)], a_recv)
     state = jnp.zeros((BODY, HD), F32)
     run = [jnp.zeros((1, HD), F32)] * HEADS
     inner, passed, row_decay = [], [], []
@@ -257,8 +249,7 @@
     for i in range(rows // HD - 1):
         attend(1, i)
 
-    for j in range(1, nx):
-        x_copy(j).wait_recv()
+    await_all(xbuf.at[pl.ds(0, nx - 1)], x_recv)
     base = jnp.zeros((BODY, HD), F32)
     for j in range(nx - 1):
         own = read_decay(xbuf[j, BODY:MSG, :])
@@ -271,15 +262,15 @@
 
     attend(1, rows // HD - 1)
 
-    others(range(NZ), p_wait)
+    await_all(pbuf.at[pl.ds(0, NZ - 1)], p_recv)
 
     @pl.when(early)
     def _():
-        lax.fori_loop(0, x * NZ, count(r_wait), 0)
         since = per_head([sum(jnp.where(j < z, own[h], 0.0) for j, own in enumerate(row_decay)) for h in range(HEADS)])
         entering[...] = jnp.zeros_like(entering)
 
         def join(row):
+            await_all(direct.at[pl.ds(row * NZ, NZ)], r_recv.at[row])
             own = jnp.exp(per_head(read_decay(direct[row * NZ, BODY:MSG, :])))
             for j in range(NZ):
                 entering[j] = entering[j] * own + direct[row * NZ + j, :BODY, :].astype(F32)
@@ -303,7 +294,7 @@
     def n_copy(g):
         p = pl.ds(groups[g][0], groups[g][1])
         return pltpu.make_async_remote_copy(
-            nbuf.at[p, 1 - core], nrecv.at[p], core_send.at[1 + g], core_recv.at[1 + g],
+            nbuf.at[p, 1 - core], nrecv.at[p], core_send.at[1], core_recv.at[1 + g],
             device_id=mate, device_id_type=MESH,
         )
 
@@ -323,7 +314,7 @@
 
     def h_copy(d, k):
         return pltpu.make_async_remote_copy(
-            nbuf.at[0, lax.rem(core + k, 2)], head.at[d, k], h_send.at[d, k], h_recv.at[d, k],
+            nbuf.at[0, lax.rem(core + k, 2)], head.at[d, k], h_send, h_recv,
             device_id=(up, down)[d] if k == 0 else aslant[d], device_id_type=MESH,
         )
 
@@ -361,7 +352,7 @@
         source = part.at[index(b), owed(b, upward, hop)] if hop == 0 else rbuf.at[index(b), slot(b, upward, hop - 1)]
         at = slot(b, upward, hop)
         return pltpu.make_async_remote_copy(
-            source, rbuf.at[index(b), at], ring_send.at[index(b), at], ring_recv.at[index(b), at],
+            source, rbuf.at[index(b), at], ring_send, ring_recv.at[index(b), at],
             device_id=up if upward else down, device_id_type=MESH,
         )
 
@@ -374,8 +365,6 @@
         lax.fori_loop(start, end, step, 0)
 
     groups = [(0, 3), (3, ny - 3)]
-    for p in range(ABSORB - 1):
-        hand_on(p)
     norm(0)
     for d in (0, 1):
         for k in (0, 1):
@@ -396,17 +385,15 @@
 
     each(functools.partial(first, absorbed=True), 0, ABSORB)
     each(functools.partial(first, absorbed=False), ABSORB)
-    hand_on(ABSORB - 1)
+    hand_on()
     rest = lhs_of(1)
-    for d in (0, 1):
-        for k in (0, 1):
-            h_copy(d, k).wait_recv()
+    await_all(head, h_recv)
     heads = [jnp.concatenate([head[d, 0], head[d, 1]], axis=1) for d in (0, 1)]
 
+    await_all(wnext.at[:, pl.ds(kdim, kdim)], f_recv)
     for p in range(ABSORB):
         for d in (0, 1):
             b, upward = (p, d), d == 0
-            f_copy(d, p).wait_recv()
             theirs = dot(heads[d], wnext[d, :, p * block : (p + 1) * block])
             own = part[index(b), owed(b, upward, 1)].astype(F32)
             rbuf[index(b), slot(b, upward, 0)] = (theirs + own).astype(BF16)
@@ -439,31 +426,17 @@
 
     each(finish)
 
-    for j in range(1, NZ):
-        a_copy(j).wait_send()
-    others(range(NZ), lambda i: p_copy(i).wait_send())
-    lax.fori_loop(0, directs, count(lambda t: r_copy(t).wait_send()), 0)
-    for j in range(1, nx):
-        x_copy(j).wait_send()
+    await_all(sbuf.at[pl.ds(0, NZ - 1)], a_send)
+    await_all(psend.at[pl.ds(0, NZ - 1)], p_send)
+    await_all(xbuf.at[pl.ds(0, nx - 1)], x_send)
+    lax.fori_loop(0, nx - 1 - x, count(lambda d: await_all(direct.at[pl.ds(0, EARLY)], r_send.at[d])), 0)
     w_copy.wait_send()
-    for g in range(len(groups)):
-        n_copy(g).wait_send()
-
-    for d in (0, 1):
-        for p in range(ABSORB):
-            y_copy(d, p).wait_send()
-            f_copy(d, p).wait_send()
-        for k in (0, 1):
-            h_copy(d, k).wait_send()
-
-    def drain(b, absorbed):
-        for upward in (True, False):
-            for hop in range(hops(b, upward)):
-                if not (absorbed and hop == 0 and upward == longer(b)):
-                    chain(b, upward, hop).wait_send()
-
-    each(functools.partial(drain, absorbed=True), 0, ABSORB)
-    each(functools.partial(drain, absorbed=False), ABSORB)
+    await_all(nrecv, core_send.at[1])
+    await_all(wnext.at[:, pl.ds(0, kdim)], y_send)
+    await_all(wnext.at[:, pl.ds(0, kdim)], f_send)
+    await_all(head, h_send)
+    sent = STREAMS * (ny - 1) - 2 * ABSORB
+    await_all(wbuf.at[pl.ds(0, sent * mine // STREAMS)], ring_send)
 
 
 def solution(mesh):
@@ -485,8 +458,7 @@
             out_specs=vmem,
             scratch_shapes=[
                 pltpu.VMEM(q_spikes.shape, BF16),
-                pltpu.VMEM(q_spikes.shape, BF16),
-                pltpu.VMEM(q_spikes.shape, BF16),
+                pltpu.VMEM((2, *q_spikes.shape), BF16),
                 pltpu.VMEM((HEADS, rows), F32),
                 pltpu.VMEM((1, kdim), F32),
                 pltpu.VMEM((2 * kdim, width), BF16),
@@ -507,9 +479,8 @@
                 pltpu.VMEM((2, 2, mine, kdim), BF16),
                 pltpu.VMEM((STREAMS, ny, mine, wide), BF16),
                 pltpu.VMEM((STREAMS, ny - 1, mine, wide), BF16),
-                dma((7,)), dma((3,)), dma((3,)), dma((NZ,)), dma((NZ,)), dma((nx,)), dma((nx,)),
-                dma((NZ,)), dma((NZ,)), dma(((nx - 1) * EARLY,)), dma(((nx - 1) * NZ,)), dma((2, ABSORB)), dma((2, ABSORB)), dma((2, ABSORB)), dma((2, ABSORB)), dma((2, 2)), dma((2, 2)),
-                dma((STREAMS, ny - 1)), dma((STREAMS, ny - 1)),
+                dma((6,)), dma((2,)), dma((3,)), dma, dma, dma, dma, dma, dma, dma((nx - 1,)), dma((nx - 1,)),
+                dma, dma, dma, dma, dma, dma, dma, dma((STREAMS, ny - 1)),
             ],
             compiler_params=pltpu.CompilerParams(
                 collective_id=0, has_side_effects=True, vmem_limit_bytes=48 * 2**20

time: 51.3 us -> 50.3 us (0.981)
  Pallas kernels: 50.4 us -> 49.5 us
    pallas_call x1, Pallas kernels: 50.4 us -> 49.5 us  [shards(): pl.pallas_call(functools.partial(kernel, nx, ny), out_shape=pltpu.VMEM(re...]
where the time goes in v5:
time: 50.3 us; the launch traced here: 50.2 us
  Pallas kernels  49.5 us (98%)
  local copies, waits for them, and re-layouts  0.71 us (1%)
    pallas_call x1, Pallas kernels, shards(): pl.pallas_call(functools.partial(kernel, nx, ny), out_shape=pltpu.VMEM(re...  49.5 us

profile of v5, /device:TPU:1, one launch (start us, length us, event | category | flops | bytes accessed | tf_op | source)
XLA Modules:
  0.0 50.2 jit_solution(6017813912932918425)
XLA Ops:
  0.0 49.5 %shard_map.73 = bf16[32,4096]{1,0:T(8,128)(2,1)S(1)} custom-call(bf16[512,256]{1,0:T(8,128)(2,1)} %q_in.1, bf16[512,256]{1,0:T(8,128)(2,1)} %k_in.1, bf16[512,256]{1,0:T(8,128)(2,1)} %v_in.1, f32[2,512]{1,0:T(2,128)} %bitcast.2, f32[1,256]{1,0:T(1,128)} %bitcast.3, bf16[256,4096]{1,0:T(8,128)(2,1)} %w_ref.1, bf16[32,4096]{1,0:T(8,128)(2,1)} %res_ref.1), custom_call_target="tpu_custom_call" | custom-call | tf_op jit(solution)/shard_map/pallas_call | solution.py:454
  49.5 0.7 %copy.9 = bf16[32,4096]{1,0:T(8,128)(2,1)} copy(bf16[32,4096]{1,0:T(8,128)(2,1)S(1)} %shard_map.73) | data formatting | bytes 524288

commit v6 on v5

--- a/solution.py
+++ b/solution.py
@@ -166,7 +166,7 @@
     def r_copy(t):
         to = (x + 1 + t // EARLY) * NZ + lax.rem(t, EARLY)
         return pltpu.make_async_remote_copy(
-            xsend, direct.at[ctx], r_send.at[t // EARLY], r_recv.at[x], device_id=(to, ex), device_id_type=MESH
+            xsend.at[pl.ds(0, BODY)], direct.at[ctx], r_send.at[t // EARLY], r_recv.at[x], device_id=(to, ex), device_id_type=MESH
         )
 
     def count(body):
@@ -271,9 +271,9 @@
 
         def join(row):
             await_all(direct.at[pl.ds(row * NZ, NZ)], r_recv.at[row])
-            own = jnp.exp(per_head(read_decay(direct[row * NZ, BODY:MSG, :])))
+            own = jnp.exp(per_head(read_decay(xbuf[row, BODY:MSG, :])))
             for j in range(NZ):
-                entering[j] = entering[j] * own + direct[row * NZ + j, :BODY, :].astype(F32)
+                entering[j] = entering[j] * own + direct[row * NZ + j].astype(F32)
 
         lax.fori_loop(0, x, count(join), 0)
         factor = jnp.exp(since)
@@ -469,7 +469,7 @@
                 pltpu.VMEM((nx, MSG, HD), BF16),
                 pltpu.VMEM((NZ, BODY, HD), BF16),
                 pltpu.VMEM((NZ, BODY, HD), BF16),
-                pltpu.VMEM(((nx - 1) * NZ, MSG, HD), BF16),
+                pltpu.VMEM(((nx - 1) * NZ, BODY, HD), BF16),
                 pltpu.VMEM((NZ, BODY, HD), F32),
                 pltpu.VMEM((rows, HEADS * HD), F32),
                 pltpu.VMEM((rows, HD), F32),

time: 50.3 us -> 49.4 us (0.982); the launches traced: 50.2 us -> 48.6 us
  Pallas kernels: 49.5 us -> 47.9 us
    pallas_call x1, Pallas kernels: 49.5 us -> 47.9 us  [shards(): pl.pallas_call(functools.partial(kernel, nx, ny), out_shape=pltpu.VMEM(re...]
where the time goes in v6:
time: 49.4 us; the launch traced here: 48.6 us
  Pallas kernels  47.9 us (97%)
  local copies, waits for them, and re-layouts  0.71 us (1%)
    pallas_call x1, Pallas kernels, shards(): pl.pallas_call(functools.partial(kernel, nx, ny), out_shape=pltpu.VMEM(re...  47.9 us

profile of v6, /device:TPU:1, one launch (start us, length us, event | category | flops | bytes accessed | tf_op | source)
XLA Modules:
  0.0 48.6 jit_solution(17968531229651179951)
XLA Ops:
  0.0 47.9 %shard_map.73 = bf16[32,4096]{1,0:T(8,128)(2,1)S(1)} custom-call(bf16[512,256]{1,0:T(8,128)(2,1)} %q_in.1, bf16[512,256]{1,0:T(8,128)(2,1)} %k_in.1, bf16[512,256]{1,0:T(8,128)(2,1)} %v_in.1, f32[2,512]{1,0:T(2,128)} %bitcast.2, f32[1,256]{1,0:T(1,128)} %bitcast.3, bf16[256,4096]{1,0:T(8,128)(2,1)} %w_ref.1, bf16[32,4096]{1,0:T(8,128)(2,1)} %res_ref.1), custom_call_target="tpu_custom_call" | custom-call | tf_op jit(solution)/shard_map/pallas_call | solution.py:454
  47.9 0.7 %copy.9 = bf16[32,4096]{1,0:T(8,128)(2,1)} copy(bf16[32,4096]{1,0:T(8,128)(2,1)S(1)} %shard_map.73) | data formatting | bytes 524288

commit v7 on v6

--- a/solution.py
+++ b/solution.py
@@ -176,7 +176,7 @@
 
         return step
 
-    for j in range(1, NZ):
+    for j in sorted(range(1, NZ), key=lambda j: -min(j, NZ - j)):
         a_copy(j).start()
     w_copy = pltpu.make_async_remote_copy(
         w_ref, wbuf.at[pl.ds(kdim, kdim)], core_send.at[0], core_recv.at[0], device_id=mate, device_id_type=MESH
@@ -238,7 +238,8 @@
         run = [a + b for a, b in zip(run, own)]
     xsend[:BODY, :] = state.astype(BF16)
     xsend[BODY:, :] = decay_tile(run)
-    lax.fori_loop(0, directs, count(lambda t: r_copy(t).start()), 0)
+    for t in reversed(range((nx - 1) * EARLY)):
+        pl.when(t < directs)(lambda t=t: r_copy(t).start())
     for j in range(EARLY):
         psend[j] = inner[j].astype(BF16)
     others(range(EARLY), lambda i: p_copy(i).start())

time: 49.4 us -> 48.9 us (0.990)
  no operation moved by 1% of the time
where the time goes in v7:
time: 48.9 us; the launch traced here: 48.3 us
  Pallas kernels  47.6 us (97%)
  local copies, waits for them, and re-layouts  0.71 us (1%)
    pallas_call x1, Pallas kernels, shards(): pl.pallas_call(functools.partial(kernel, nx, ny), out_shape=pltpu.VMEM(re...  47.6 us

profile of v7, /device:TPU:1, one launch (start us, length us, event | category | flops | bytes accessed | tf_op | source)
XLA Modules:
  0.0 48.3 jit_solution(10739471135673374781)
XLA Ops:
  0.0 47.6 %shard_map.73 = bf16[32,4096]{1,0:T(8,128)(2,1)S(1)} custom-call(bf16[512,256]{1,0:T(8,128)(2,1)} %q_in.1, bf16[512,256]{1,0:T(8,128)(2,1)} %k_in.1, bf16[512,256]{1,0:T(8,128)(2,1)} %v_in.1, f32[2,512]{1,0:T(2,128)} %bitcast.2, f32[1,256]{1,0:T(1,128)} %bitcast.3, bf16[256,4096]{1,0:T(8,128)(2,1)} %w_ref.1, bf16[32,4096]{1,0:T(8,128)(2,1)} %res_ref.1), custom_call_target="tpu_custom_call" | custom-call | tf_op jit(solution)/shard_map/pallas_call | solution.py:455
  47.6 0.7 %copy.9 = bf16[32,4096]{1,0:T(8,128)(2,1)} copy(bf16[32,4096]{1,0:T(8,128)(2,1)S(1)} %shard_map.73) | data formatting | bytes 524288

commit v8 on v7

--- a/solution.py
+++ b/solution.py
@@ -243,7 +243,7 @@
     for j in range(EARLY):
         psend[j] = inner[j].astype(BF16)
     others(range(EARLY), lambda i: p_copy(i).start())
-    for j in range(1, nx):
+    for j in sorted(range(1, nx), key=lambda j: -min(j, nx - j)):
         x_copy(j).start()
     xbuf[x] = xsend[...]
 
@@ -258,7 +258,8 @@
         base = jnp.where(j < x, later, base)
     for j in range(EARLY, NZ):
         psend[j] = (inner[j] + base * jnp.exp(per_head(passed[j]))).astype(BF16)
-    others(range(EARLY, NZ), lambda i: p_copy(i).start())
+    for j in sorted(range(1, NZ), key=lambda j: -min(j, NZ - j)):
+        pl.when(z_peer(j) >= EARLY)(lambda j=j: p_copy(z_peer(j)).start())
     pbuf[z] = psend[z]
 
     attend(1, rows // HD - 1)

time: 48.9 us -> 48.7 us (level)
  no operation moved by 1% of the time
where the time goes in v8:
time: 48.7 us; the launch traced here: 48.3 us
  Pallas kernels  47.6 us (98%)
  local copies, waits for them, and re-layouts  0.71 us (1%)
    pallas_call x1, Pallas kernels, shards(): pl.pallas_call(functools.partial(kernel, nx, ny), out_shape=pltpu.VMEM(re...  47.6 us

profile of v8, /device:TPU:1, one launch (start us, length us, event | category | flops | bytes accessed | tf_op | source)
XLA Modules:
  0.0 48.3 jit_solution(6711863645063179340)
XLA Ops:
  0.0 47.6 %shard_map.73 = bf16[32,4096]{1,0:T(8,128)(2,1)S(1)} custom-call(bf16[512,256]{1,0:T(8,128)(2,1)} %q_in.1, bf16[512,256]{1,0:T(8,128)(2,1)} %k_in.1, bf16[512,256]{1,0:T(8,128)(2,1)} %v_in.1, f32[2,512]{1,0:T(2,128)} %bitcast.2, f32[1,256]{1,0:T(1,128)} %bitcast.3, bf16[256,4096]{1,0:T(8,128)(2,1)} %w_ref.1, bf16[32,4096]{1,0:T(8,128)(2,1)} %res_ref.1), custom_call_target="tpu_custom_call" | custom-call | tf_op jit(solution)/shard_map/pallas_call | solution.py:456
  47.6 0.7 %copy.9 = bf16[32,4096]{1,0:T(8,128)(2,1)} copy(bf16[32,4096]{1,0:T(8,128)(2,1)S(1)} %shard_map.73) | data formatting | bytes 524288
